TPU v7x, 32 devices: a whole 2x2x4 slice. The times are simulated.
32 devices in a mesh: groups: 2 (over y), virt: 4 (over z), pair: 2 (over x), sub: 2 (over core).
Axes of the slice: x: 2, y: 2, z: 4, core: 2. Of those that a mesh axis runs over, the one named last changes fastest.
Arguments:
- amplitudes: bfloat16 [3840, 2048], P(('groups', 'pair', 'virt'), 'sub'), parts along dimension 0, may hold values from -4 to 4
- driver: bfloat16 [3840, 2048], P(('groups', 'pair', 'virt'), 'sub'), parts along dimension 0, may hold values from -6 to 6
- integrals: bfloat16 [4096, 2048], P(('groups', 'sub'), 'virt'), parts along dimension 0, may hold values from -0.125 to 0.125
- pair_energy: float32 [3840], P(('groups', 'pair', 'virt')), parts along dimension 0, may hold values from -1.5 to -0.5
- col_energy: float32 [4096], P(('groups', 'sub')), parts along dimension 0, may hold values from 0.5 to 3
- tile_irrep: int32 [32], P(('groups', 'sub')), parts along dimension 0, may hold values from 0 to 3
- pair_irrep: int32 [3840], P(('groups', 'pair', 'virt')), parts along dimension 0, may hold values from 0 to 3, as said below
- mirror_slot: int32 [3840], P(('groups', 'pair', 'virt')), parts along dimension 0, may hold values from 0 to 239, as said below
Outputs:
- amplitudes_next: float32 [3840, 2048], P(('groups', 'pair', 'virt'), 'sub'), parts along dimension 0
There are 2 independent parts, one for each index of `groups`. A program takes and returns all parts, laid end to end along the dimension named above; each array names one. Nothing has to cross between parts.
Inputs may be any that keep to these rules, and one draw needn't show every extreme that they name: `mirror_slot`: within each pair of mirrored blocks (block b and block b + 4) the map is a permutation whose entries point back to each other. `pair_irrep`: A pair and its mirror carry the same label.
All inputs are finite; a program needn't handle non-finite values.
Results may differ from a plain program's by a relative error of at most 0.00088.
Values may be sent and summed in bfloat16 or wider, within the bound.
No kernel may reach another device: no remote copies, remote signals or barrier semaphores. Data moves between devices by JAX's collectives and lax.ppermute only.
A program may use at most 64 MiB of HBM per device.

v0:
```python
import functools

import jax
import jax.numpy as jnp
from jax import lax
from jax.experimental import pallas as pl
from jax.experimental.pallas import tpu as pltpu
from jax.sharding import PartitionSpec as P

ITERS = 2
TILE = 128
IRREPS = 4
PIECES = 2
CHUNK = 16
CAPS = (5, 6, 7, 8)
VMEM_BYTES = 20 * 1024 * 1024


def from_partner(value, axis, apart):
    return lax.ppermute(value, axis, [(i, i ^ 1 << apart) for i in range(lax.axis_size(axis))])


def contract(blocks, integrals):
    places, z, sub = lax.axis_size("virt"), lax.axis_index("virt"), lax.axis_index("sub")
    width = integrals.shape[1]
    whole = jnp.zeros((integrals.shape[0], places * width), integrals.dtype)
    for apart in range(places):
        slab = integrals
        if apart:
            slab = lax.ppermute(
                integrals, "virt", [(i, (i + apart) % places) for i in range(places)]
            )
        at = lax.rem(z - apart + places, places) * width
        whole = lax.dynamic_update_slice(whole, slab, (0, at))
    total = jnp.dot(blocks[0], whole, preferred_element_type=jnp.float32)
    half = total.shape[1] // 2
    mine = lax.dynamic_slice_in_dim(total, sub * half, half, 1)
    theirs = lax.dynamic_slice_in_dim(total, (1 - sub) * half, half, 1)
    return mine + from_partner(theirs, "sub", 0)


def dense_plan(
    amplitudes, driver, integrals, pair_energy, col_energy, tile_irrep, pair_irrep, mirror_slot
):
    col_irrep = jnp.repeat(tile_irrep, TILE)
    occupied = pair_irrep[:, None] == col_irrep[None, :]
    energy_gap = col_energy[None, :] - pair_energy[:, None]
    driver_wide = driver.astype(jnp.float32)
    partner_bit = lax.axis_size("pair").bit_length() - 2
    current = jnp.where(occupied, amplitudes, jnp.zeros((), amplitudes.dtype))
    updated = driver_wide
    for iteration in range(ITERS):
        ladder = contract((current,), integrals)
        mirror_block = from_partner(ladder, "pair", partner_bit)
        symmetric = ladder + jnp.take(mirror_block, mirror_slot, axis=0)
        updated = jnp.where(
            occupied, (driver_wide + symmetric) / energy_gap, jnp.zeros((), jnp.float32)
        )
        current = updated.astype(jnp.bfloat16)
    return updated


class Plan:
    def __init__(self, tiles, slab_tiles, places, cap):
        self.tiles = tiles
        self.half = tiles // 2
        self.slab = slab_tiles
        self.places = places
        self.near = places // 2
        self.part = -(-cap // 2)
        self.cap = 2 * self.part

    def pieces(self, rows):
        first = max(self.half // 2, self.part * TILE // rows + 1)
        return (first, self.half - first)


def split(value, size):
    assert size & (size - 1) == 0
    return value >> (size.bit_length() - 1), value & (size - 1)


def tile_at(index):
    return pl.ds(pl.multiple_of(index * TILE, TILE), TILE)


def all_labels(plan, own, other, sub, labels):
    for i in range(plan.half):
        labels[sub * plan.half + i] = own[i]
        labels[(1 - sub) * plan.half + i] = other[i]


def list_tiles(plan, labels, slab, spots):
    for n in range(plan.cap):
        spots[n] = 0
    count = jnp.int32(0)
    for j in range(plan.slab):
        here = labels[slab * plan.slab + j]
        for k in range(plan.tiles):
            spots[count] = j * plan.tiles + k
            count += (labels[k] == here).astype(jnp.int32)
    spots[count] = 0


def list_kernel(plans, own, other, place, level_ref, spots_ref, labels, spots, sizes):
    plan = plans[-1]
    all_labels(plan, own, other, place[2], labels)
    for k in range(plan.tiles):
        sizes[k] = 0
    for k in range(plan.tiles):
        sizes[labels[k]] += 1
    most = jnp.int32(0)
    for i in range(plan.places):
        needed = jnp.int32(0)
        for j in range(plan.slab):
            needed += sizes[labels[i * plan.slab + j]]
        most = jnp.maximum(most, needed)
    level = jnp.int32(0)
    for each in plans:
        level += (most > each.cap).astype(jnp.int32)
    level_ref[0] = level
    list_tiles(plan, labels, place[0], spots)
    for n in range(plan.cap):
        spots_ref[n] = spots[n]


def pack_kernel(plan, spots, place, mine_ref, their_ref, *send_refs):
    slab, side, sub = place[0], place[1], place[2]
    is_near = slab // plan.near == sub
    for i, to_ref in enumerate(send_refs):
        first = jnp.where(is_near, i, side) * plan.part
        for n in range(plan.part):
            spot = spots[first + n]
            j, k = split(spot, plan.tiles)
            core, row = split(k, plan.half)
            rows, cols = tile_at(row), tile_at(j)
            to_ref[n * TILE : (n + 1) * TILE, :] = jnp.where(
                core == sub, mine_ref[rows, cols], their_ref[rows, cols]
            )


def column(row):
    n = row.shape[1]
    here = lax.broadcasted_iota(jnp.int32, (n, n), 0) == lax.broadcasted_iota(jnp.int32, (n, n), 1)
    return jnp.sum(jnp.where(here, row.astype(jnp.float32), 0.0), axis=1, keepdims=True)


def mirror_table(slot_row):
    n = slot_row.shape[1]
    slots = column(slot_row).astype(jnp.int32)
    return lax.broadcasted_iota(jnp.int32, (n, n), 1) == slots


class Rows:
    def __init__(self, rows, cols):
        self.rows = rows
        self.sorted = rows + IRREPS * CHUNK
        self.tiles = cols // TILE
        self.most = -(-rows // CHUNK)
        self.cap = self.tiles * self.most * 2 // 5
        self.energy = -(-rows // TILE)
        self.sent = (2 * self.cap + self.energy) * CHUNK


def list_chunks(shape, own, label_row, sizes, spots):
    firsts, first = [], jnp.int32(0)
    for g in range(IRREPS):
        count = jnp.sum(jnp.where(label_row == g, 1.0, 0.0)).astype(jnp.int32)
        chunks = (count + CHUNK - 1) // CHUNK
        sizes[g], sizes[IRREPS + g] = first, chunks
        firsts.append(first * CHUNK)
        first += chunks
    for n in range(shape.cap):
        spots[n] = 0
    total = jnp.int32(0)
    for j in range(shape.tiles):
        first, chunks = sizes[own[j]], sizes[IRREPS + own[j]]
        for c in range(shape.most):
            spots[total] = j * TILE + first + c
            total += (c < chunks).astype(jnp.int32)
    spots[total] = 0
    return total, firsts


def first_of(labels, firsts):
    value = jnp.zeros(labels.shape, jnp.float32)
    for g, first in enumerate(firsts):
        value = jnp.where(labels == g, first.astype(jnp.float32), value)
    return value


def chunk_at(spot):
    j, chunk = split(spot, TILE)
    return pl.ds(pl.multiple_of(chunk * CHUNK, CHUNK), CHUNK), tile_at(j)


def rows_kernel(
    shape, own, amps_ref, driver_ref, label_row, energy_row, out_ref, full_ref, amps, drivers, sizes,
    spots,
):
    n = shape.rows
    total, firsts = list_chunks(shape, own, label_row[...], sizes, spots)
    full_ref[0] = (total > shape.cap).astype(jnp.int32)
    labels = column(label_row[...]).astype(jnp.int32)
    above = lax.broadcasted_iota(jnp.int32, (n, n), 0) < lax.broadcasted_iota(jnp.int32, (n, n), 1)
    rank = jnp.where((labels == label_row[...]) & above, 1.0, 0.0).sum(axis=0, keepdims=True)
    spot_row = (rank + first_of(label_row[...], firsts)).astype(jnp.int32)
    order = lax.broadcasted_iota(jnp.int32, (shape.sorted, n), 0) == spot_row
    order = order.astype(jnp.bfloat16)
    for to_ref, from_ref in ((amps, amps_ref), (drivers, driver_ref)):
        to_ref[...] = jnp.dot(order, from_ref[...], preferred_element_type=jnp.float32).astype(
            to_ref.dtype
        )
    for i in range(shape.cap):
        rows, cols = chunk_at(spots[i])
        out_ref[i * CHUNK : (i + 1) * CHUNK, :] = amps[rows, cols]
        out_ref[(shape.cap + i) * CHUNK : (shape.cap + i + 1) * CHUNK, :] = drivers[rows, cols]

    rest = jnp.broadcast_to(energy_row[...], (CHUNK, n))
    at = lax.broadcasted_iota(jnp.int32, (CHUNK, n), 0)
    terms = jnp.zeros((CHUNK, n), jnp.float32)
    for i in range(3):
        term = rest.astype(jnp.bfloat16).astype(jnp.float32)
        terms = jnp.where(at == i, term, terms)
        rest = rest - term
    for i in range(shape.energy):
        width = min(TILE, n - i * TILE)
        first = (2 * shape.cap + i) * CHUNK
        out_ref[first : first + CHUNK, :] = jnp.zeros((CHUNK, TILE), out_ref.dtype)
        out_ref[first : first + CHUNK, :width] = terms[:, i * TILE : i * TILE + width].astype(
            out_ref.dtype
        )


def mirror_kernel(shape, pieces, whole, own, amps_ref, bundle_ref, slot_row, label_row, energy_row, *refs):
    if whole:
        amps, drivers, *cur_refs, mirror_driver_ref, columns_ref = refs
    else:
        *cur_refs, mirror_driver_ref, columns_ref, amps, drivers, sizes, spots = refs
    rows = shape.rows
    table = mirror_table(slot_row[...])
    row_label = column(label_row[...])
    if whole:
        weights = table
    else:
        total, firsts = list_chunks(shape, own, label_row[...], sizes, spots)
        amps[...] = jnp.zeros_like(amps)
        drivers[...] = jnp.zeros_like(drivers)
        for i in range(shape.cap):
            at = chunk_at(spots[i])
            amps[at] = bundle_ref[i * CHUNK : (i + 1) * CHUNK, :]
            drivers[at] = bundle_ref[(shape.cap + i) * CHUNK : (shape.cap + i + 1) * CHUNK, :]
        slots = column(slot_row[...]).astype(jnp.int32)
        before = (row_label == label_row[...].astype(jnp.float32)) & (slot_row[...] < slots)
        rank = jnp.where(before, 1.0, 0.0).sum(axis=1, keepdims=True)
        spot = (rank + first_of(row_label, firsts)).astype(jnp.int32)
        weights = lax.broadcasted_iota(jnp.int32, (rows, shape.sorted), 1) == spot
    weights = weights.astype(jnp.bfloat16)
    mirrored = jnp.dot(weights, amps[...], preferred_element_type=jnp.float32)
    zero = jnp.zeros((), amps_ref.dtype)
    for j in range(shape.tiles):
        cols = slice(j * TILE, (j + 1) * TILE)
        cur_ref, first = (cur_refs[0], 0) if j < pieces[0] else (cur_refs[1], pieces[0])
        at = slice((j - first) * TILE, (j - first + 1) * TILE)
        occupied = row_label == own[j].astype(jnp.float32)
        cur_ref[:rows, at] = jnp.where(occupied, amps_ref[:, cols], zero)
        cur_ref[rows:, at] = jnp.where(occupied, mirrored[:, cols], 0.0).astype(cur_ref.dtype)
    mirror_driver_ref[...] = jnp.dot(
        weights, drivers[...], preferred_element_type=jnp.float32
    ).astype(mirror_driver_ref.dtype)
    mirror_energy = jnp.zeros((rows, 1), jnp.float32)
    for i in range(shape.energy):
        width = min(TILE, rows - i * TILE)
        first = (2 * shape.cap + i) * CHUNK
        terms = bundle_ref[first : first + CHUNK, :width].astype(jnp.float32)
        other_energy = (terms[0:1] + terms[1:2]) + terms[2:3]
        here = table[:, i * TILE : i * TILE + width]
        mirror_energy += jnp.where(here, other_energy, 0.0).sum(axis=1, keepdims=True)
    for i, value in enumerate((row_label, column(energy_row[...]), mirror_energy)):
        columns_ref[i * rows : (i + 1) * rows, :] = jnp.broadcast_to(value, (rows, TILE))


def bounds(plan, core, first, count):
    return pl.ds(pl.multiple_of(core * plan.half * TILE + first, TILE), count)


def first_column(plan, place, i):
    here = lax.rem(place[0], plan.near)
    return lax.rem(here + 2 + i, plan.near) * plan.slab * TILE


def slot_of_near(plan, turn):
    return (-(turn // 2 + 1) - 2) % plan.near


def slot_of_far(plan, turn):
    return (-turn - 2) % plan.near


def turns_for(plan, slots):
    return (
        [t for t in range(2 * (plan.near - 1)) if slot_of_near(plan, t) in slots],
        [t for t in range(plan.near) if slot_of_far(plan, t) in slots],
    )


def fill(plan, slots, own, other, place, near_got, far_got, swapped, ints_ref, labels, spots):
    z, side, sub = place[0], place[1], place[2]
    here = lax.rem(z, plan.near)
    ints_ref[...] = jnp.zeros_like(ints_ref)
    all_labels(plan, own, other, sub, labels)
    near_turns, far_turns = turns_for(plan, slots)

    def put(slot, n, value):
        spot = spots[n]
        j, k = split(spot, plan.tiles)
        ints_ref[tile_at(k), tile_at((slot - slots[0]) * plan.slab + j)] = value

    def list_slot(slot):
        slab = sub * plan.near + lax.rem(here + 2 + slot, plan.near)
        list_tiles(plan, labels, slab, spots)

    @pl.when(z // plan.near == sub)
    def _():
        for turn in near_turns:
            slot = slot_of_near(plan, turn)
            if turn % 2 == 0:
                list_slot(slot)
            for n in range(plan.part):
                tile = near_got[turn][n * TILE : (n + 1) * TILE, :]
                put(slot, turn % 2 * plan.part + n, tile)

    @pl.when(z // plan.near != sub)
    def _():
        for turn in far_turns:
            slot = slot_of_far(plan, turn)
            list_slot(slot)
            for n in range(plan.part):
                rows = slice(n * TILE, (n + 1) * TILE)
                put(slot, side * plan.part + n, far_got[turn][rows, :])
                put(slot, (1 - side) * plan.part + n, swapped[turn][rows, :])


def new_current(plan, slots, own, place, pieces, ints_ref, driver, mirror_driver, columns, col_energy,
                cur_ref):
    rows = driver.shape[0]
    width = plan.slab * TILE
    wide = min(width, 2 * TILE)
    terms = []
    for i, piece in enumerate(pieces):
        core = place[2] if i < PIECES else 1 - place[2]
        sizes = [tiles * TILE for tiles in plan.pieces(2 * rows)]
        terms.append((piece, bounds(plan, core, i % PIECES * sizes[0], sizes[i % PIECES])))
    for slot in slots:
        first = first_column(plan, place, slot)
        for c in range(0, width, wide):
            cols = slice((slot - slots[0]) * width + c, (slot - slots[0]) * width + c + wide)
            total = None
            for piece, at in terms:
                term = jnp.dot(piece[...], ints_ref[at, cols], preferred_element_type=jnp.float32)
                total = term if total is None else total + term
            sym = total[:rows] + total[rows:]
            for t in range(0, wide, TILE):
                at = pl.ds(pl.multiple_of(first + c + t, TILE), TILE)
                occupied = columns[:rows] == own[(first + c + t) // TILE].astype(jnp.float32)
                for i, source in enumerate((driver, mirror_driver)):
                    gap = col_energy[:, at] - columns[(i + 1) * rows : (i + 2) * rows]
                    new = (source[:, at].astype(jnp.float32) + sym[:, t : t + TILE]) / gap
                    new = jnp.where(occupied, new, 0.0)
                    cur_ref[i * rows : (i + 1) * rows, cols.start + t : cols.start + t + TILE] = (
                        new.astype(cur_ref.dtype)
                    )


def take_turns(turns, refs):
    refs = list(refs)
    return [{t: refs.pop(0) for t in each} for each in (turns[0], turns[1], turns[1])]


def early_kernel(plan, turns, *refs):
    own, other, place, mine_ref, their_ref = refs[:5]
    pieces, refs = refs[5 : 5 + 2 * PIECES], refs[5 + 2 * PIECES :]
    came = take_turns(turns, refs[4:-4])
    ints_ref, cur_ref, labels, spots = refs[-4:]
    slots = range(plan.near - 1)
    width = plan.slab * TILE
    fill(plan, slots, own, other, place, *came, ints_ref, labels, spots)

    @pl.when(place[0] // plan.near == place[2])
    def _():
        cols = slice((plan.near - 2) * width, (plan.near - 1) * width)
        ints_ref[bounds(plan, place[2], 0, plan.half * TILE), cols] = mine_ref[...]
        ints_ref[bounds(plan, 1 - place[2], 0, plan.half * TILE), cols] = their_ref[...]

    new_current(plan, slots, own, place, pieces, ints_ref, *refs[:4], cur_ref)


def late_kernel(plan, turns, *refs):
    own, other, place = refs[:3]
    pieces, refs = refs[3 : 3 + 2 * PIECES], refs[3 + 2 * PIECES :]
    came = take_turns(turns, refs[4:-4])
    ints_ref, cur_ref, labels, spots = refs[-4:]
    slots = range(plan.near - 1, plan.near)
    fill(plan, slots, own, other, place, *came, ints_ref, labels, spots)
    new_current(plan, slots, own, place, pieces, ints_ref, *refs[:4], cur_ref)


def product(plan, place, terms, ints_ref, cols):
    width = plan.slab * TILE
    total = None
    for cur_ref, core, slots in terms:
        for slot in slots:
            at = slice((slot - slots[0]) * width, (slot - slots[0] + 1) * width)
            rows = bounds(plan, core, first_column(plan, place, slot), width)
            term = jnp.dot(
                cur_ref[:, at], ints_ref[rows, cols], preferred_element_type=jnp.float32
            )
            total = term if total is None else total + term
    half = total.shape[0] // 2
    return total[:half] + total[half:]


def blocks(plan, count):
    width = plan.slab * TILE
    wide = min(width, 2 * TILE)
    return [slice(c, c + wide) for c in range(0, count * width, wide)]


def early_part_kernel(plan, place, a_mine, a_their, ints_a, sym_ref):
    a = range(plan.near - 1)
    terms = [(a_mine, place[2], a), (a_their, 1 - place[2], a)]
    for cols in blocks(plan, plan.near - 1):
        sym_ref[:, cols] = product(plan, place, terms, ints_a, cols)


def part_kernel(plan, place, a_mine, a_their, b_mine, ints_a, ints_b, early_ref, sym_ref):
    a, b = range(plan.near - 1), range(plan.near - 1, plan.near)
    terms = [(b_mine, place[2], b)]
    for cols in blocks(plan, plan.near - 1):
        sym_ref[:, cols] = early_ref[:, cols] + product(plan, place, terms, ints_a, cols)
    terms = [(a_mine, place[2], a), (a_their, 1 - place[2], a), (b_mine, place[2], b)]
    width = (plan.near - 1) * plan.slab * TILE
    for cols in blocks(plan, 1):
        sym_ref[:, width + cols.start : width + cols.stop] = product(plan, place, terms, ints_b, cols)


def last_kernel(plan, own, place, b_their, ints_a, ints_b, sym_ref, driver, columns, col_energy, out_ref,
                new_ref, sems):
    rows = driver.shape[0]
    terms = [(b_their, 1 - place[2], range(plan.near - 1, plan.near))]
    width = plan.slab * TILE
    copies = []
    for c, cols in enumerate(blocks(plan, plan.near)):
        slot = cols.start // width
        ints_ref, start = (ints_b, cols.start - slot * width) if slot == plan.near - 1 else (ints_a, cols.start)
        wide = cols.stop - cols.start
        sym = sym_ref[:, cols] + product(plan, place, terms, ints_ref, slice(start, start + wide))
        first = first_column(plan, place, slot) + cols.start - slot * width
        for t in range(0, wide, TILE):
            at = pl.ds(pl.multiple_of(first + t, TILE), TILE)
            occupied = columns[:rows] == own[(first + t) // TILE].astype(jnp.float32)
            gap = col_energy[:, at] - columns[rows : 2 * rows]
            new = (driver[:, at].astype(jnp.float32) + sym[:, t : t + TILE]) / gap
            new_ref[:, cols.start + t : cols.start + t + TILE] = jnp.where(occupied, new, 0.0)
        at = pl.ds(pl.multiple_of(first, TILE), wide)
        copy = pltpu.make_async_copy(new_ref.at[:, cols], out_ref.at[:, at], sems.at[c])
        copy.start()
        copies.append(copy)
    for copy in copies:
        copy.wait()


def call(kernel, smem, vmem, outs, scratch=(), anywhere=(), flag=False, flops=0, to_hbm=False):
    moved = sum(v.size * v.dtype.itemsize for v in vmem)
    in_smem, in_vmem = pl.BlockSpec(memory_space=pltpu.SMEM), pl.BlockSpec(memory_space=pltpu.VMEM)
    in_any = pl.BlockSpec(memory_space=pl.ANY)
    return pl.pallas_call(
        kernel,
        out_shape=list(outs) + [jax.ShapeDtypeStruct((1,), jnp.int32)] * flag,
        in_specs=[in_smem] * len(smem) + [in_vmem] * len(vmem) + [in_any] * len(anywhere),
        out_specs=[pl.BlockSpec(memory_space=pltpu.HBM) if to_hbm else in_vmem] * len(outs) + [in_smem] * flag,
        scratch_shapes=scratch,
        compiler_params=pltpu.CompilerParams(vmem_limit_bytes=VMEM_BYTES),
        cost_estimate=pl.CostEstimate(flops=0, bytes_accessed=0, transcendentals=0),
    )(*smem, *vmem, *anywhere)


def body(
    amplitudes, driver, integrals, pair_energy, col_energy, tile_irrep, pair_irrep, mirror_slot
):
    places, sides = lax.axis_size("virt"), lax.axis_size("pair")
    partner_bit = sides.bit_length() - 2
    rows, half_cols = amplitudes.shape
    slab_tiles = integrals.shape[1] // TILE
    plans = [
        Plan(2 * half_cols // TILE, slab_tiles, places, per_tile * slab_tiles)
        for per_tile in CAPS
    ]
    plan = plans[-1]
    z, sub = lax.axis_index("virt"), lax.axis_index("sub")
    side = (lax.axis_index("pair") >> partner_bit) & 1
    place = jnp.stack([z, side, sub]).astype(jnp.int32)

    def like(shape, dtype=integrals.dtype):
        return jax.ShapeDtypeStruct(shape, dtype)

    other_irrep = from_partner(tile_irrep, "sub", 0)
    their_ints = from_partner(integrals, "sub", 0)

    label_row, slot_row, energy_row = pair_irrep[None, :], mirror_slot[None, :], pair_energy[None, :]
    shape = Rows(rows, half_cols)
    sort_scratch = [pltpu.VMEM((shape.sorted, half_cols), amplitudes.dtype)] * 2 + [
        pltpu.SMEM((2 * IRREPS,), jnp.int32),
        pltpu.SMEM((shape.tiles * shape.most + 1,), jnp.int32),
    ]
    bundle, rows_full = call(
        functools.partial(rows_kernel, shape),
        (tile_irrep,),
        (amplitudes, driver, label_row, energy_row),
        [like((shape.sent, TILE))],
        sort_scratch,
        flag=True,
    )

    lists = [pltpu.SMEM((plan.tiles,), jnp.int32), pltpu.SMEM((plan.slab * plan.tiles + 1,), jnp.int32)]
    level, spots = list_tiles_of(plans, lists, tile_irrep, other_irrep, place, bundle)

    def sparse(index):
        return sparse_plan(
            plans[index], spots, place, lists, shape, sort_scratch,
            other_irrep, their_ints, bundle, rows_full, amplitudes, driver, integrals, label_row,
            slot_row, energy_row, col_energy, tile_irrep,
        )

    def dense():
        return dense_plan(
            amplitudes, driver, integrals, pair_energy, col_energy, tile_irrep, pair_irrep,
            mirror_slot,
        )

    branches = [functools.partial(sparse, index) for index in range(len(plans))] + [dense]
    return lax.switch(level[0], branches)


def list_tiles_of(plans, lists, own, other, place, after):
    smem = pl.BlockSpec(memory_space=pltpu.SMEM)

    def kernel(own, other, place, after_ref, *refs):
        list_kernel(plans, own, other, place, *refs)

    return pl.pallas_call(
        kernel,
        out_shape=[
            jax.ShapeDtypeStruct((1,), jnp.int32),
            jax.ShapeDtypeStruct((plans[-1].cap,), jnp.int32),
        ],
        in_specs=[smem] * 3 + [pl.BlockSpec(memory_space=pl.ANY)],
        out_specs=[smem] * 2,
        scratch_shapes=lists + [pltpu.SMEM((plans[-1].tiles,), jnp.int32)],
    )(own, other, place, after)


def sparse_plan(
    plan, spots, place, lists, shape, sort_scratch, other_irrep, their_ints, bundle, rows_full,
    amplitudes, driver, integrals, label_row, slot_row, energy_row, col_energy, tile_irrep,
):
    places, sides = lax.axis_size("virt"), lax.axis_size("pair")
    partner_bit = sides.bit_length() - 2
    rows, half_cols = amplitudes.shape

    def like(shape, dtype=integrals.dtype):
        return jax.ShapeDtypeStruct(shape, dtype)

    def over_pair(value):
        return from_partner(value, "pair", partner_bit)

    sends = call(
        functools.partial(pack_kernel, plan),
        (spots, place),
        (integrals, their_ints),
        [like((plan.part * TILE, TILE))] * 2,
    )

    near = plan.near
    got = []
    for turn in range(max(2 * (near - 1), near)):
        pairs = []
        for i in range(places):
            half, at = i // near, i % near
            if turn < 2 * (near - 1):
                to = half * near + (at + turn // 2 + 1) % near
                pairs.append((2 * i + half, 2 * to + half))
            if turn < near:
                to = (1 - half) * near + (at + turn) % near
                pairs.append((2 * i + 1 - half, 2 * to + half))
        got.append(lax.ppermute(sends[turn % 2], ("virt", "sub"), pairs))
    across = []
    for i in range(places):
        for j in range(sides):
            far = 1 - i // near
            across.append(((i * sides + j) * 2 + far, (i * sides + (j ^ 1 << partner_bit)) * 2 + far))
    near_got, far_got = got, got[:near]
    swapped = [lax.ppermute(value, ("virt", "pair", "sub"), across) for value in far_got]

    other_bundle = over_pair(bundle)
    energy = col_energy[None, :]

    def mirror(whole, more=()):
        return tuple(call(
            functools.partial(mirror_kernel, shape, plan.pieces(2 * rows), whole),
            (tile_irrep,),
            (amplitudes, other_bundle, slot_row, label_row, energy_row, *more),
            [like((2 * rows, tiles * TILE)) for tiles in plan.pieces(2 * rows)]
            + [like((rows, half_cols)), like((3 * rows, TILE), jnp.float32)],
            () if whole else sort_scratch,
        ))

    *cur_mine, mirror_driver, columns = lax.cond(
        rows_full[0] > 0,
        lambda: mirror(True, (over_pair(amplitudes), over_pair(driver))),
        lambda: mirror(False),
    )
    cur_their = [from_partner(piece, "sub", 0) for piece in cur_mine]

    width = plan.slab * TILE
    near_cols, flops = (near - 1) * width, 2 * 2 * rows * plan.tiles * TILE * width
    common = (*cur_mine, *cur_their, driver, mirror_driver, columns, energy)

    def came(turns):
        near_turns, far_turns = turns
        values = [near_got[t] for t in near_turns] + [far_got[t] for t in far_turns]
        return values + [swapped[t] for t in far_turns]

    turns = turns_for(plan, range(near - 1))
    ints_a, a_mine = call(
        functools.partial(early_kernel, plan, turns),
        (tile_irrep, other_irrep, place),
        (integrals, their_ints, *common, *came(turns)),
        [like((plan.tiles * TILE, near_cols)), like((2 * rows, near_cols))],
        lists,
        flops=flops * (near - 1),
    )
    a_their = from_partner(a_mine, "sub", 0)
    (early,) = call(
        functools.partial(early_part_kernel, plan),
        (place,),
        (a_mine, a_their, ints_a),
        [like((rows, near_cols), jnp.float32)],
        flops=flops // 2,
    )
    turns = turns_for(plan, range(near - 1, near))
    ints_b, b_mine = call(
        functools.partial(late_kernel, plan, turns),
        (tile_irrep, other_irrep, place),
        (*common, *came(turns)),
        [like((plan.tiles * TILE, width)), like((2 * rows, width))],
        lists,
        flops=flops,
    )
    b_their = from_partner(b_mine, "sub", 0)
    (sym,) = call(
        functools.partial(part_kernel, plan),
        (place,),
        (a_mine, a_their, b_mine, ints_a, ints_b, early),
        [like((rows, half_cols), jnp.float32)],
        flops=flops,
    )
    return call(
        functools.partial(last_kernel, plan),
        (tile_irrep, place),
        (b_their, ints_a, ints_b, sym, driver, columns, energy),
        [like((rows, half_cols), jnp.float32)],
        [pltpu.VMEM((rows, half_cols), jnp.float32),
         pltpu.SemaphoreType.DMA((len(blocks(plan, near)),))],
        flops=flops // 2,
        to_hbm=True,
    )[0]


def solution(mesh):
    return jax.shard_map(
        body,
        mesh=mesh,
        in_specs=(
            P(("groups", "pair", "virt"), "sub"),
            P(("groups", "pair", "virt"), "sub"),
            P(("groups", "sub"), "virt"),
            P(("groups", "pair", "virt")),
            P(("groups", "sub")),
            P(("groups", "sub")),
            P(("groups", "pair", "virt")),
            P(("groups", "pair", "virt")),
        ),
        out_specs=P(("groups", "pair", "virt"), "sub"),
        check_vma=False,
    )
```

profile of v0, /device:TPU:0, one launch (start us, length us, event | category | flops | bytes accessed | tf_op | source)
XLA Modules:
  0.0 44.2 jit_solution(6608809049954520493)
XLA Ops:
  0.0 0.5 %collective-permute-start.52 = (bf16[1024,512]{1,0:T(8,128)(2,1)}, bf16[1024,512]{1,0:T(8,128)(2,1)S(1)}, u32[]{:S(2)}, u32[]{:S(2)}) collective-permute-start(bf16[1024,512]{1,0:T(8,128)(2,1)} %param.25), channel_id=1, source_target_pairs={{0,1},{1,0},{2,3},{3,2},{4,5},{5,4},{6,7},{7,6},{8,9},{9,8},{10,11... | collective-permute-start | bytes 3145736 | tf_op jit(solution)/shard_map/ppermute | solution.py:20
  0.5 0.1 collective-permute-start.51
  0.5 2.4 %shard_map.87 = (bf16[1568,128]{1,0:T(8,128)(2,1)S(1)}, s32[1]{0:T(128)}) custom-call(s32[8]{0:T(128)} %own.3, bf16[240,1024]{1,0:T(8,128)(2,1)} %amps_ref.1, bf16[240,1024]{1,0:T(8,128)(2,1)} %driver_ref.1, s32[1,240]{1,0:T(1,128)} %bitcast.34, f32[1,240]{1,0:T(1,128)} %bitcast.39), custom_call_target="tpu_custom_call" | custom-call | tf_op jit(solution)/shard_map/pallas_call | solution.py:477
  2.9 0.1 pad_add_fusion.place
  3.0 0.0 collective-permute-done.51.other
  3.0 1.5 %shard_map.88 = (s32[1]{0:T(128)}, s32[32]{0:T(128)S(1)}) custom-call(s32[8]{0:T(128)} %own.3, s32[8]{0:T(128)S(1)} %collective-permute-done.51.other, s32[3]{0:T(128)S(1)} %pad_add_fusion.place, bf16[1568,128]{1,0:T(8,128)(2,1)S(1)} %get-tuple-element.408.after_ref), custom_call_target="tpu_custom_call" | custom-call | tf_op jit(solution)/shard_map/pallas_call | solution.py:551
  5.2 0.0 collective-permute-done.52
  5.2 38.8 %conditional.5 = (f32[240,1024]{1,0:T(8,128)}) conditional(s32[]{:T(128)} %bitcast.18, (s32[1]{0:T(128)}, bf16[1568,128]{1,0:T(8,128)(2,1)S(1)}, s32[240]{0:T(256)}, s32[8]{0:T(128)}, bf16[240,1024]{1,0:T(8,128)(2,1)}, /*index=5*/s32[1,240]{1,0:T(1,128)}, f32[1,240]{1,0:T(1,128)}, bf16[240,1024]{1,0:T(8,128)(2,1)}, ...), branch_computations={%region_0.0_spmd, %region_3.0_spmd, %region_6.0_spmd, %region_9.0_... | conditional | flops 2018430080 | bytes 106204832 | solution.py:542
  5.2 0.0 copy-start.5
  5.2 0.0 copy-start.35
  5.2 3.0 %collective-permute-start.2 = (bf16[1568,128]{1,0:T(8,128)(2,1)S(1)}, bf16[1568,128]{1,0:T(8,128)(2,1)S(1)}, u32[]{:S(2)}, u32[]{:S(2)}) collective-permute-start(bf16[1568,128]{1,0:T(8,128)(2,1)S(1)} %get-tuple-element.266), channel_id=1, source_target_pairs={{0,2},{2,0},{1,3},{3,1},{4,6},{6,4},{5,7},{7,5},{8,10},{10,8},{9,1... | collective-permute-start | bytes 1204232 | tf_op jit(solution)/shard_map/cond/branch_0_fun/ppermute | solution.py:20
  8.2 1.5 %branch_0_fun.11 = (bf16[1280,128]{1,0:T(8,128)(2,1)S(1)}, bf16[1280,128]{1,0:T(8,128)(2,1)S(1)}) custom-call(s32[32]{0:T(128)S(1)} %get-tuple-element.276.spots, s32[3]{0:T(128)S(1)} %get-tuple-element.262.place.refs_2_, bf16[1024,512]{1,0:T(8,128)(2,1)} %get-tuple-element.277.mine_ref.refs_3_, bf16[1024,512]{1,0:T(8,128)(2,1)S(1)} %get-tuple-element.278.their_ref.refs_4_), custom_call_target="tpu_custom_call" | custom-call | tf_op jit(solution)/shard_map/cond/branch_0_fun/pallas_call | solution.py:477
  9.7 1.6 %collective-permute-start.5 = (bf16[1280,128]{1,0:T(8,128)(2,1)S(1)}, bf16[1280,128]{1,0:T(8,128)(2,1)S(1)}, u32[]{:S(2)}, u32[]{:S(2)}) collective-permute-start(bf16[1280,128]{1,0:T(8,128)(2,1)S(1)} %get-tuple-element.279), channel_id=1, source_target_pairs={{0,4},{1,8},{4,0},{5,12},{9,13},{8,1},{13,9},{12,5},{2,6},{3,10},{... | collective-permute-start | bytes 983048 | tf_op jit(solution)/shard_map/cond/branch_0_fun/ppermute | solution.py:596
  11.4 0.4 %collective-permute-start.6 = (bf16[1280,128]{1,0:T(8,128)(2,1)S(1)}, bf16[1280,128]{1,0:T(8,128)(2,1)S(1)}, u32[]{:S(2)}, u32[]{:S(2)}) collective-permute-start(bf16[1280,128]{1,0:T(8,128)(2,1)S(1)} %get-tuple-element.280), channel_id=1, source_target_pairs={{0,4},{1,12},{4,0},{5,8},{9,13},{8,5},{13,9},{12,1},{2,6},{3,14},{... | collective-permute-start | bytes 983048 | tf_op jit(solution)/shard_map/cond/branch_0_fun/ppermute | solution.py:596
  12.4 5.3 %collective-permute-done.2 = bf16[1568,128]{1,0:T(8,128)(2,1)S(1)} collective-permute-done((bf16[1568,128]{1,0:T(8,128)(2,1)S(1)}, bf16[1568,128]{1,0:T(8,128)(2,1)S(1)}, u32[]{:S(2)}, u32[]{:S(2)}) %collective-permute-start.2) | collective-permute-done | bytes 401440 | tf_op jit(solution)/shard_map/cond/branch_0_fun/ppermute | solution.py:20
  17.7 3.2 %conditional = ((bf16[480,512]{1,0:T(8,128)(2,1)}, bf16[480,512]{1,0:T(8,128)(2,1)}, bf16[240,1024]{1,0:T(8,128)(2,1)}, f32[720,128]{1,0:T(8,128)})) conditional(s32[]{:T(128)} %bitcast, (s32[8]{0:T(128)}, bf16[240,1024]{1,0:T(8,128)(2,1)}, bf16[1568,128]{1,0:T(8,128)(2,1)S(1)}, s32[1,240]{1,0:T(1,128)}, s32[1,240]{1,0:T(1,128)}, ...), branch_computations={%region_1.0_spmd, %region_2.0_spmd} | conditional | bytes 5537908 | solution.py:618
  17.7 3.2 %branch_0_fun.10 = (bf16[480,512]{1,0:T(8,128)(2,1)}, bf16[480,512]{1,0:T(8,128)(2,1)}, bf16[240,1024]{1,0:T(8,128)(2,1)}, f32[720,128]{1,0:T(8,128)}) custom-call(s32[8]{0:T(128)} %get-tuple-element.248.own, bf16[240,1024]{1,0:T(8,128)(2,1)} %get-tuple-element.249.amps_ref, bf16[1568,128]{1,0:T(8,128)(2,1)S(1)} %get-tuple-element.250.bundle_ref, ...), custom_call_target="tpu_custom_call" | custom-call | tf_op jit(solution)/shard_map/cond/branch_0_fun/cond/branch_0_fun/pallas_call | solution.py:477
  20.9 0.1 collective-permute-start.3
  21.0 0.5 %collective-permute-start.4 = (bf16[480,512]{1,0:T(8,128)(2,1)}, bf16[480,512]{1,0:T(8,128)(2,1)S(1)}, u32[]{:S(2)}, u32[]{:S(2)}) collective-permute-start(bf16[480,512]{1,0:T(8,128)(2,1)} %get-tuple-element.272.refs_4_.refs_6_), channel_id=1, source_target_pairs={{0,1},{1,0},{2,3},{3,2},{4,5},{5,4},{6,7},{7,6},{8,9},{9,8},{10,11... | collective-permute-start | bytes 1474568 | tf_op jit(solution)/shard_map/cond/branch_0_fun/ppermute | solution.py:20
  21.5 0.0 collective-permute-done.5.refs_11_.refs_13_
  21.5 0.7 %collective-permute-start.9 = (bf16[1280,128]{1,0:T(8,128)(2,1)S(1)}, bf16[1280,128]{1,0:T(8,128)(2,1)S(1)}, u32[]{:S(2)}, u32[]{:S(2)}) collective-permute-start(bf16[1280,128]{1,0:T(8,128)(2,1)S(1)} %collective-permute-done.5.refs_11_.refs_13_), channel_id=1, source_target_pairs={{1,3},{3,1},{5,7},{7,5},{8,10},{10,8},{12,14},{14,12},{17,19},{19,... | collective-permute-start | bytes 983048 | tf_op jit(solution)/shard_map/cond/branch_0_fun/ppermute | solution.py:603
  22.2 3.9 %collective-permute-done.6.refs_12_.refs_13_ = bf16[1280,128]{1,0:T(8,128)(2,1)S(1)} collective-permute-done((bf16[1280,128]{1,0:T(8,128)(2,1)S(1)}, bf16[1280,128]{1,0:T(8,128)(2,1)S(1)}, u32[]{:S(2)}, u32[]{:S(2)}) %collective-permute-start.6) | collective-permute-done | bytes 327712 | tf_op jit(solution)/shard_map/cond/branch_0_fun/ppermute | solution.py:596
  26.1 0.7 %collective-permute-start.7 = (bf16[1280,128]{1,0:T(8,128)(2,1)S(1)}, bf16[1280,128]{1,0:T(8,128)(2,1)S(1)}, u32[]{:S(2)}, u32[]{:S(2)}) collective-permute-start(bf16[1280,128]{1,0:T(8,128)(2,1)S(1)} %collective-permute-done.6.refs_12_.refs_13_), channel_id=1, source_target_pairs={{1,3},{3,1},{5,7},{7,5},{8,10},{10,8},{12,14},{14,12},{17,19},{19,... | collective-permute-start | bytes 983048 | tf_op jit(solution)/shard_map/cond/branch_0_fun/ppermute | solution.py:603
  26.8 0.0 collective-permute-done.9.refs_14_
  26.8 0.0 collective-permute-done.4.refs_6_.refs_8_
  26.9 3.5 %branch_0_fun.13 = (bf16[2048,512]{1,0:T(8,128)(2,1)S(1)}, bf16[480,512]{1,0:T(8,128)(2,1)S(1)}) custom-call(s32[8]{0:T(128)} %get-tuple-element.261.refs_0_.own, s32[8]{0:T(128)S(1)} %get-tuple-element.263.refs_1_, s32[3]{0:T(128)S(1)} %get-tuple-element.262.place.refs_2_, bf16[1024,512]{1,0:T(8,128)(2,1)S(1)} %copy-done.5, bf16[1024,512]{1,0:T(8,128)(2,1)} %copy-done.9, ...), custom_call_target="tpu_custom_call" | custom-call | tf_op jit(solution)/shard_map/cond/branch_0_fun/pallas_call | solution.py:477
  30.4 3.9 %collective-permute-start.10 = (bf16[480,512]{1,0:T(8,128)(2,1)S(1)}, bf16[480,512]{1,0:T(8,128)(2,1)S(1)}, u32[]{:S(2)}, u32[]{:S(2)}) collective-permute-start(bf16[480,512]{1,0:T(8,128)(2,1)S(1)} %get-tuple-element.284.a_mine), channel_id=1, source_target_pairs={{0,1},{1,0},{2,3},{3,2},{4,5},{5,4},{6,7},{7,6},{8,9},{9,8},{10,11... | collective-permute-start | bytes 1474568 | tf_op jit(solution)/shard_map/cond/branch_0_fun/ppermute | solution.py:20
  34.4 2.4 %branch_0_fun.12 = (bf16[2048,512]{1,0:T(8,128)(2,1)S(1)}, bf16[480,512]{1,0:T(8,128)(2,1)S(1)}) custom-call(s32[8]{0:T(128)S(1)} %copy-done.41, s32[8]{0:T(128)S(1)} %get-tuple-element.263.refs_1_, s32[3]{0:T(128)S(1)} %get-tuple-element.262.place.refs_2_, bf16[480,512]{1,0:T(8,128)(2,1)S(1)} %copy-done.19, bf16[480,512]{1,0:T(8,128)(2,1)S(1)} %copy-done.20, ...), custom_call_target="tpu_custom_call" | custom-call | tf_op jit(solution)/shard_map/cond/branch_0_fun/pallas_call | solution.py:477
  36.8 1.5 %collective-permute-start.8 = (bf16[480,512]{1,0:T(8,128)(2,1)S(1)}, bf16[480,512]{1,0:T(8,128)(2,1)S(1)}, u32[]{:S(2)}, u32[]{:S(2)}) collective-permute-start(bf16[480,512]{1,0:T(8,128)(2,1)S(1)} %get-tuple-element.281.b_mine), channel_id=1, source_target_pairs={{0,1},{1,0},{2,3},{3,2},{4,5},{5,4},{6,7},{7,6},{8,9},{9,8},{10,11... | collective-permute-start | bytes 1474568 | tf_op jit(solution)/shard_map/cond/branch_0_fun/ppermute | solution.py:20
  38.3 1.2 %branch_0_fun.14.early_ref = f32[240,512]{1,0:T(8,128)S(1)} custom-call(s32[3]{0:T(128)S(1)} %get-tuple-element.262.place.refs_2_, bf16[480,512]{1,0:T(8,128)(2,1)S(1)} %get-tuple-element.284.a_mine, bf16[480,512]{1,0:T(8,128)(2,1)S(1)} %collective-permute-done.10.a_their, bf16[2048,512]{1,0:T(8,128)(2,1)S(1)} %get-tuple-element.282.ints_a), custom_call_target="tpu_custom_call" | custom-call | tf_op jit(solution)/shard_map/cond/branch_0_fun/pallas_call | solution.py:477
  39.5 1.7 %branch_0_fun.15.sym_ref = f32[240,1024]{1,0:T(8,128)S(1)} custom-call(s32[3]{0:T(128)S(1)} %get-tuple-element.262.place.refs_2_, bf16[480,512]{1,0:T(8,128)(2,1)S(1)} %get-tuple-element.284.a_mine, bf16[480,512]{1,0:T(8,128)(2,1)S(1)} %collective-permute-done.10.a_their, bf16[480,512]{1,0:T(8,128)(2,1)S(1)} %get-tuple-element.281.b_mine, ...), custom_call_target="tpu_custom_call" | custom-call | tf_op jit(solution)/shard_map/cond/branch_0_fun/pallas_call | solution.py:477
  41.2 2.2 %branch_0_fun.16 = f32[240,1024]{1,0:T(8,128)} custom-call(s32[8]{0:T(128)S(1)} %copy-done.41, s32[3]{0:T(128)S(1)} %get-tuple-element.262.place.refs_2_, bf16[480,512]{1,0:T(8,128)(2,1)S(1)} %collective-permute-done.8.b_their, bf16[2048,512]{1,0:T(8,128)(2,1)S(1)} %get-tuple-element.282.ints_a, bf16[2048,512]{1,0:T(8,128)(2,1)S(1)} %get-tuple-element.283.ints_b, ...), custom_call_target="tpu_custom_call" | custom-call | tf_op jit(solution)/shard_map/cond/branch_0_fun/pallas_call | solution.py:477
  (20 shorter events, 0.0 us)
Async XLA Ops:
  0.0 5.2 %collective-permute-start.52 = (bf16[1024,512]{1,0:T(8,128)(2,1)}, bf16[1024,512]{1,0:T(8,128)(2,1)S(1)}, u32[]{:S(2)}, u32[]{:S(2)}) collective-permute-start(bf16[1024,512]{1,0:T(8,128)(2,1)} %param.25), channel_id=1, source_target_pairs={{0,1},{1,0},{2,3},{3,2},{4,5},{5,4},{6,7},{7,6},{8,9},{9,8},{10,11... | collective-permute-start | bytes 3145736 | tf_op jit(solution)/shard_map/ppermute | solution.py:20
  0.5 2.6 %collective-permute-start.51 = (s32[8]{0:T(128)}, s32[8]{0:T(128)S(1)}, u32[]{:S(2)}, u32[]{:S(2)}) collective-permute-start(s32[8]{0:T(128)} %own.3), channel_id=1, source_target_pairs={{0,1},{1,0},{2,3},{3,2},{4,5},{5,4},{6,7},{7,6},{8,9},{9,8},{10,11... | collective-permute-start | bytes 104 | tf_op jit(solution)/shard_map/ppermute | solution.py:20
  5.2 4.5 %copy-start.9 = (bf16[1024,512]{1,0:T(8,128)(2,1)}, bf16[1024,512]{1,0:T(8,128)(2,1)S(1)}, u32[]{:S(2)}) copy-start(bf16[1024,512]{1,0:T(8,128)(2,1)S(1)} %get-tuple-element.278.their_ref.refs_4_) | copy-start | bytes 3145732 | tf_op jit(solution)/shard_map/cond
  5.2 21.6 %copy-start.5 = (bf16[1024,512]{1,0:T(8,128)(2,1)S(1)}, bf16[1024,512]{1,0:T(8,128)(2,1)}, u32[]{:S(2)}) copy-start(bf16[1024,512]{1,0:T(8,128)(2,1)} %get-tuple-element.277.mine_ref.refs_3_) | copy-start | bytes 3145732 | tf_op jit(solution)/shard_map/cond
  5.2 21.6 %copy-start.35 = (f32[1024]{0:T(1024)S(1)}, f32[1024]{0:T(1024)}, u32[]{:S(2)}) copy-start(f32[1024]{0:T(1024)} %get-tuple-element.275) | copy-start | bytes 12292 | tf_op jit(solution)/shard_map/cond
  5.2 12.5 %collective-permute-start.2 = (bf16[1568,128]{1,0:T(8,128)(2,1)S(1)}, bf16[1568,128]{1,0:T(8,128)(2,1)S(1)}, u32[]{:S(2)}, u32[]{:S(2)}) collective-permute-start(bf16[1568,128]{1,0:T(8,128)(2,1)S(1)} %get-tuple-element.266), channel_id=1, source_target_pairs={{0,2},{2,0},{1,3},{3,1},{4,6},{6,4},{5,7},{7,5},{8,10},{10,8},{9,1... | collective-permute-start | bytes 1204232 | tf_op jit(solution)/shard_map/cond/branch_0_fun/ppermute | solution.py:20
  9.7 11.8 %collective-permute-start.5 = (bf16[1280,128]{1,0:T(8,128)(2,1)S(1)}, bf16[1280,128]{1,0:T(8,128)(2,1)S(1)}, u32[]{:S(2)}, u32[]{:S(2)}) collective-permute-start(bf16[1280,128]{1,0:T(8,128)(2,1)S(1)} %get-tuple-element.279), channel_id=1, source_target_pairs={{0,4},{1,8},{4,0},{5,12},{9,13},{8,1},{13,9},{12,5},{2,6},{3,10},{... | collective-permute-start | bytes 983048 | tf_op jit(solution)/shard_map/cond/branch_0_fun/ppermute | solution.py:596
  11.4 14.8 %collective-permute-start.6 = (bf16[1280,128]{1,0:T(8,128)(2,1)S(1)}, bf16[1280,128]{1,0:T(8,128)(2,1)S(1)}, u32[]{:S(2)}, u32[]{:S(2)}) collective-permute-start(bf16[1280,128]{1,0:T(8,128)(2,1)S(1)} %get-tuple-element.280), channel_id=1, source_target_pairs={{0,4},{1,12},{4,0},{5,8},{9,13},{8,5},{13,9},{12,1},{2,6},{3,14},{... | collective-permute-start | bytes 983048 | tf_op jit(solution)/shard_map/cond/branch_0_fun/ppermute | solution.py:596
  17.7 16.7 %copy-start = (bf16[240,1024]{1,0:T(8,128)(2,1)S(1)}, bf16[240,1024]{1,0:T(8,128)(2,1)}, u32[]{:S(2)}) copy-start(bf16[240,1024]{1,0:T(8,128)(2,1)} %get-tuple-element.270.refs_7_.refs_9_.driver) | copy-start | bytes 1474564 | tf_op jit(solution)/shard_map/cond
  17.7 16.7 %copy-start.41 = (s32[8]{0:T(128)S(1)}, s32[8]{0:T(128)}, u32[]{:S(2)}) copy-start(s32[8]{0:T(128)} %get-tuple-element.261.refs_0_.own) | copy-start | bytes 100 | tf_op jit(solution)/shard_map/cond
  20.9 13.5 %copy-start.15 = (f32[720,128]{1,0:T(8,128)S(1)}, f32[720,128]{1,0:T(8,128)}, u32[]{:S(2)}) copy-start(f32[720,128]{1,0:T(8,128)} %get-tuple-element.274.refs_9_.refs_11_.columns) | copy-start | bytes 1105924 | tf_op jit(solution)/shard_map/cond
  20.9 13.5 %copy-start.19 = (bf16[480,512]{1,0:T(8,128)(2,1)S(1)}, bf16[480,512]{1,0:T(8,128)(2,1)}, u32[]{:S(2)}) copy-start(bf16[480,512]{1,0:T(8,128)(2,1)} %get-tuple-element.271.refs_3_.refs_5_) | copy-start | bytes 1474564 | tf_op jit(solution)/shard_map/cond
  20.9 13.5 %copy-start.20 = (bf16[480,512]{1,0:T(8,128)(2,1)S(1)}, bf16[480,512]{1,0:T(8,128)(2,1)}, u32[]{:S(2)}) copy-start(bf16[480,512]{1,0:T(8,128)(2,1)} %get-tuple-element.272.refs_4_.refs_6_) | copy-start | bytes 1474564 | tf_op jit(solution)/shard_map/cond
  20.9 13.5 %copy-start.21 = (bf16[240,1024]{1,0:T(8,128)(2,1)S(1)}, bf16[240,1024]{1,0:T(8,128)(2,1)}, u32[]{:S(2)}) copy-start(bf16[240,1024]{1,0:T(8,128)(2,1)} %get-tuple-element.273.refs_8_.refs_10_) | copy-start | bytes 1474564 | tf_op jit(solution)/shard_map/cond
  20.9 5.9 %collective-permute-start.3 = (bf16[480,512]{1,0:T(8,128)(2,1)}, bf16[480,512]{1,0:T(8,128)(2,1)S(1)}, u32[]{:S(2)}, u32[]{:S(2)}) collective-permute-start(bf16[480,512]{1,0:T(8,128)(2,1)} %get-tuple-element.271.refs_3_.refs_5_), channel_id=1, source_target_pairs={{0,1},{1,0},{2,3},{3,2},{4,5},{5,4},{6,7},{7,6},{8,9},{9,8},{10,11... | collective-permute-start | bytes 1474568 | tf_op jit(solution)/shard_map/cond/branch_0_fun/ppermute | solution.py:20
  21.0 5.8 %collective-permute-start.4 = (bf16[480,512]{1,0:T(8,128)(2,1)}, bf16[480,512]{1,0:T(8,128)(2,1)S(1)}, u32[]{:S(2)}, u32[]{:S(2)}) collective-permute-start(bf16[480,512]{1,0:T(8,128)(2,1)} %get-tuple-element.272.refs_4_.refs_6_), channel_id=1, source_target_pairs={{0,1},{1,0},{2,3},{3,2},{4,5},{5,4},{6,7},{7,6},{8,9},{9,8},{10,11... | collective-permute-start | bytes 1474568 | tf_op jit(solution)/shard_map/cond/branch_0_fun/ppermute | solution.py:20
  21.5 5.3 %collective-permute-start.9 = (bf16[1280,128]{1,0:T(8,128)(2,1)S(1)}, bf16[1280,128]{1,0:T(8,128)(2,1)S(1)}, u32[]{:S(2)}, u32[]{:S(2)}) collective-permute-start(bf16[1280,128]{1,0:T(8,128)(2,1)S(1)} %collective-permute-done.5.refs_11_.refs_13_), channel_id=1, source_target_pairs={{1,3},{3,1},{5,7},{7,5},{8,10},{10,8},{12,14},{14,12},{17,19},{19,... | collective-permute-start | bytes 983048 | tf_op jit(solution)/shard_map/cond/branch_0_fun/ppermute | solution.py:603
  26.1 8.2 %collective-permute-start.7 = (bf16[1280,128]{1,0:T(8,128)(2,1)S(1)}, bf16[1280,128]{1,0:T(8,128)(2,1)S(1)}, u32[]{:S(2)}, u32[]{:S(2)}) collective-permute-start(bf16[1280,128]{1,0:T(8,128)(2,1)S(1)} %collective-permute-done.6.refs_12_.refs_13_), channel_id=1, source_target_pairs={{1,3},{3,1},{5,7},{7,5},{8,10},{10,8},{12,14},{14,12},{17,19},{19,... | collective-permute-start | bytes 983048 | tf_op jit(solution)/shard_map/cond/branch_0_fun/ppermute | solution.py:603
  30.4 7.8 %collective-permute-start.10 = (bf16[480,512]{1,0:T(8,128)(2,1)S(1)}, bf16[480,512]{1,0:T(8,128)(2,1)S(1)}, u32[]{:S(2)}, u32[]{:S(2)}) collective-permute-start(bf16[480,512]{1,0:T(8,128)(2,1)S(1)} %get-tuple-element.284.a_mine), channel_id=1, source_target_pairs={{0,1},{1,0},{2,3},{3,2},{4,5},{5,4},{6,7},{7,6},{8,9},{9,8},{10,11... | collective-permute-start | bytes 1474568 | tf_op jit(solution)/shard_map/cond/branch_0_fun/ppermute | solution.py:20
  36.8 4.5 %collective-permute-start.8 = (bf16[480,512]{1,0:T(8,128)(2,1)S(1)}, bf16[480,512]{1,0:T(8,128)(2,1)S(1)}, u32[]{:S(2)}, u32[]{:S(2)}) collective-permute-start(bf16[480,512]{1,0:T(8,128)(2,1)S(1)} %get-tuple-element.281.b_mine), channel_id=1, source_target_pairs={{0,1},{1,0},{2,3},{3,2},{4,5},{5,4},{6,7},{7,6},{8,9},{9,8},{10,11... | collective-permute-start | bytes 1474568 | tf_op jit(solution)/shard_map/cond/branch_0_fun/ppermute | solution.py:20
where the time goes:
time: 44.6 us; the launch traced here: 44.2 us
  Pallas kernels  19.6 us (44%)
  starting transfers between devices  12.9 us (29%)
  waiting for transfers between devices  9.23 us (21%)
  loops' own time  1.39 us (3%)
  between operations  0.9 us (2%)
    pallas_call x8, Pallas kernels, call(): pl.pallas_call(kernel, out_shape=list(outs) + [jax.ShapeDtypeStruct((1,),...  18.1 us
    ppermute x7, starting transfers between devices, from_partner(): lax.ppermute(value, axis, [(i, i ^ 1 << apart) for i in range(lax.axis_si...  9.5 us
    ppermute x7, waiting for transfers between devices, from_partner(): lax.ppermute(value, axis, [(i, i ^ 1 << apart) for i in range(lax.axis_si...  5.27 us
    ppermute x2, waiting for transfers between devices, sparse_plan(): got.append(lax.ppermute(sends[turn % 2], ('virt', 'sub'), pairs))  3.95 us
    ppermute x2, starting transfers between devices, sparse_plan(): got.append(lax.ppermute(sends[turn % 2], ('virt', 'sub'), pairs))  2.09 us
    pallas_call x1, Pallas kernels, list_tiles_of(): pl.pallas_call(kernel, out_shape=[jax.ShapeDtypeStruct((1,), jnp.int32),...  1.49 us
    another operation x1, loops' own time, body(): return lax.switch(level[0], branches)  1.39 us
    ppermute x2, starting transfers between devices, sparse_plan(): lax.ppermute(value, ('virt', 'pair', 'sub'), across)  1.34 us
  transfers between devices with their start and end apart: 11, of which 2 were waited for; matrix products, arithmetic and copies ran while one was open for 0% of the time, Pallas kernels for 39%

commit v1 on v0

--- a/solution.py
+++ b/solution.py
@@ -12,7 +12,7 @@
 IRREPS = 4
 PIECES = 2
 CHUNK = 16
-CAPS = (5, 6, 7, 8)
+CAPS = (5, 6, 7, 9)
 VMEM_BYTES = 20 * 1024 * 1024
 
 

time: 44.6 us -> 48.2 us (1.081)
  the two profiles are of different devices: /device:TPU:0 before, /device:TPU:21 now
where the time goes in v1:
time: 48.2 us; the launch traced here: 47.9 us
  Pallas kernels  19.7 us (41%)
  starting transfers between devices  14.5 us (30%)
  waiting for transfers between devices  11.3 us (23%)
  loops' own time  1.38 us (3%)
  between operations  0.9 us (2%)
    pallas_call x8, Pallas kernels, call(): pl.pallas_call(kernel, out_shape=list(outs) + [jax.ShapeDtypeStruct((1,),...  18.2 us
    ppermute x7, starting transfers between devices, from_partner(): lax.ppermute(value, axis, [(i, i ^ 1 << apart) for i in range(lax.axis_si...  11.5 us
    ppermute x2, waiting for transfers between devices, sparse_plan(): got.append(lax.ppermute(sends[turn % 2], ('virt', 'sub'), pairs))  5.82 us
    ppermute x7, waiting for transfers between devices, from_partner(): lax.ppermute(value, axis, [(i, i ^ 1 << apart) for i in range(lax.axis_si...  5.46 us
    ppermute x2, starting transfers between devices, sparse_plan(): got.append(lax.ppermute(sends[turn % 2], ('virt', 'sub'), pairs))  1.53 us
    ppermute x2, starting transfers between devices, sparse_plan(): lax.ppermute(value, ('virt', 'pair', 'sub'), across)  1.53 us
    pallas_call x1, Pallas kernels, list_tiles_of(): pl.pallas_call(kernel, out_shape=[jax.ShapeDtypeStruct((1,), jnp.int32),...  1.5 us
    another operation x1, loops' own time, body(): return lax.switch(level[0], branches)  1.38 us
  transfers between devices with their start and end apart: 11, of which 2 were waited for; matrix products, arithmetic and copies ran while one was open for 0% of the time, Pallas kernels for 37%

profile of v1, /device:TPU:21, one launch (start us, length us, event | category | flops | bytes accessed | tf_op | source)
XLA Modules:
  0.0 47.9 jit_solution(17810026167357773490)
XLA Ops:
  0.0 0.7 %collective-permute-start.52 = (bf16[1024,512]{1,0:T(8,128)(2,1)}, bf16[1024,512]{1,0:T(8,128)(2,1)S(1)}, u32[]{:S(2)}, u32[]{:S(2)}) collective-permute-start(bf16[1024,512]{1,0:T(8,128)(2,1)} %param.25), channel_id=1, source_target_pairs={{0,1},{1,0},{2,3},{3,2},{4,5},{5,4},{6,7},{7,6},{8,9},{9,8},{10,11... | collective-permute-start | bytes 3145736 | tf_op jit(solution)/shard_map/ppermute | solution.py:20
  0.7 2.4 %shard_map.87 = (bf16[1568,128]{1,0:T(8,128)(2,1)S(1)}, s32[1]{0:T(128)}) custom-call(s32[8]{0:T(128)} %own.3, bf16[240,1024]{1,0:T(8,128)(2,1)} %amps_ref.1, bf16[240,1024]{1,0:T(8,128)(2,1)} %driver_ref.1, s32[1,240]{1,0:T(1,128)} %bitcast.34, f32[1,240]{1,0:T(1,128)} %bitcast.39), custom_call_target="tpu_custom_call" | custom-call | tf_op jit(solution)/shard_map/pallas_call | solution.py:477
  3.1 0.1 pad_add_fusion.place
  3.2 0.0 collective-permute-done.51.other
  3.2 1.5 %shard_map.88 = (s32[1]{0:T(128)}, s32[36]{0:T(128)S(1)}) custom-call(s32[8]{0:T(128)} %own.3, s32[8]{0:T(128)S(1)} %collective-permute-done.51.other, s32[3]{0:T(128)S(1)} %pad_add_fusion.place, bf16[1568,128]{1,0:T(8,128)(2,1)S(1)} %get-tuple-element.408.after_ref), custom_call_target="tpu_custom_call" | custom-call | tf_op jit(solution)/shard_map/pallas_call | solution.py:551
  5.3 0.0 collective-permute-done.52
  5.4 42.3 %conditional.5 = (f32[240,1024]{1,0:T(8,128)}) conditional(s32[]{:T(128)} %bitcast.18, (s32[1]{0:T(128)}, bf16[1568,128]{1,0:T(8,128)(2,1)S(1)}, s32[240]{0:T(256)}, s32[8]{0:T(128)}, bf16[240,1024]{1,0:T(8,128)(2,1)}, /*index=5*/s32[1,240]{1,0:T(1,128)}, f32[1,240]{1,0:T(1,128)}, bf16[240,1024]{1,0:T(8,128)(2,1)}, ...), branch_computations={%region_0.0_spmd, %region_3.0_spmd, %region_6.0_spmd, %region_9.0_... | conditional | flops 2018430080 | bytes 106204832 | solution.py:542
  5.4 0.0 copy-start.6
  5.4 0.0 copy-start.37
  5.4 1.3 %collective-permute-start.13 = (bf16[1568,128]{1,0:T(8,128)(2,1)S(1)}, bf16[1568,128]{1,0:T(8,128)(2,1)S(1)}, u32[]{:S(2)}, u32[]{:S(2)}) collective-permute-start(bf16[1568,128]{1,0:T(8,128)(2,1)S(1)} %get-tuple-element.303), channel_id=1, source_target_pairs={{0,2},{2,0},{1,3},{3,1},{4,6},{6,4},{5,7},{7,5},{8,10},{10,8},{9,1... | collective-permute-start | bytes 1204232 | tf_op jit(solution)/shard_map/cond/branch_1_fun/ppermute | solution.py:20
  6.7 1.5 %branch_1_fun.12 = (bf16[1536,128]{1,0:T(8,128)(2,1)S(1)}, bf16[1536,128]{1,0:T(8,128)(2,1)S(1)}) custom-call(s32[36]{0:T(128)S(1)} %get-tuple-element.313.spots, s32[3]{0:T(128)S(1)} %get-tuple-element.299.place.refs_2_, bf16[1024,512]{1,0:T(8,128)(2,1)} %get-tuple-element.314.mine_ref.refs_3_, bf16[1024,512]{1,0:T(8,128)(2,1)S(1)} %get-tuple-element.315.their_ref.refs_4_), custom_call_target="tpu_custom_call" | custom-call | tf_op jit(solution)/shard_map/cond/branch_1_fun/pallas_call | solution.py:477
  8.2 1.4 %collective-permute-start.16 = (bf16[1536,128]{1,0:T(8,128)(2,1)S(1)}, bf16[1536,128]{1,0:T(8,128)(2,1)S(1)}, u32[]{:S(2)}, u32[]{:S(2)}) collective-permute-start(bf16[1536,128]{1,0:T(8,128)(2,1)S(1)} %get-tuple-element.316), channel_id=1, source_target_pairs={{0,4},{1,8},{4,0},{5,12},{9,13},{8,1},{13,9},{12,5},{2,6},{3,10},{... | collective-permute-start | bytes 1179656 | tf_op jit(solution)/shard_map/cond/branch_1_fun/ppermute | solution.py:596
  9.6 0.2 collective-permute-start.17
  10.4 5.4 %collective-permute-done.13 = bf16[1568,128]{1,0:T(8,128)(2,1)S(1)} collective-permute-done((bf16[1568,128]{1,0:T(8,128)(2,1)S(1)}, bf16[1568,128]{1,0:T(8,128)(2,1)S(1)}, u32[]{:S(2)}, u32[]{:S(2)}) %collective-permute-start.13) | collective-permute-done | bytes 401440 | tf_op jit(solution)/shard_map/cond/branch_1_fun/ppermute | solution.py:20
  15.8 3.2 %conditional.1 = ((bf16[480,512]{1,0:T(8,128)(2,1)}, bf16[480,512]{1,0:T(8,128)(2,1)}, bf16[240,1024]{1,0:T(8,128)(2,1)}, f32[720,128]{1,0:T(8,128)})) conditional(s32[]{:T(128)} %bitcast.3, (s32[8]{0:T(128)}, bf16[240,1024]{1,0:T(8,128)(2,1)}, bf16[1568,128]{1,0:T(8,128)(2,1)S(1)}, s32[1,240]{1,0:T(1,128)}, s32[1,240]{1,0:T(1,128)}, ...), branch_computations={%region_4.0_spmd, %region_5.0_spmd} | conditional | bytes 5537908 | solution.py:618
  15.8 3.2 %branch_0_fun.17 = (bf16[480,512]{1,0:T(8,128)(2,1)}, bf16[480,512]{1,0:T(8,128)(2,1)}, bf16[240,1024]{1,0:T(8,128)(2,1)}, f32[720,128]{1,0:T(8,128)}) custom-call(s32[8]{0:T(128)} %get-tuple-element.285.own, bf16[240,1024]{1,0:T(8,128)(2,1)} %get-tuple-element.286.amps_ref, bf16[1568,128]{1,0:T(8,128)(2,1)S(1)} %get-tuple-element.287.bundle_ref, ...), custom_call_target="tpu_custom_call" | custom-call | tf_op jit(solution)/shard_map/cond/branch_1_fun/cond/branch_0_fun/pallas_call | solution.py:477
  19.1 1.4 %collective-permute-start.14 = (bf16[480,512]{1,0:T(8,128)(2,1)}, bf16[480,512]{1,0:T(8,128)(2,1)S(1)}, u32[]{:S(2)}, u32[]{:S(2)}) collective-permute-start(bf16[480,512]{1,0:T(8,128)(2,1)} %get-tuple-element.308.refs_3_.refs_5_), channel_id=1, source_target_pairs={{0,1},{1,0},{2,3},{3,2},{4,5},{5,4},{6,7},{7,6},{8,9},{9,8},{10,11... | collective-permute-start | bytes 1474568 | tf_op jit(solution)/shard_map/cond/branch_1_fun/ppermute | solution.py:20
  20.5 0.1 collective-permute-start.15
  20.6 0.0 collective-permute-done.16.refs_11_.refs_13_
  20.6 0.7 %collective-permute-start.20 = (bf16[1536,128]{1,0:T(8,128)(2,1)S(1)}, bf16[1536,128]{1,0:T(8,128)(2,1)S(1)}, u32[]{:S(2)}, u32[]{:S(2)}) collective-permute-start(bf16[1536,128]{1,0:T(8,128)(2,1)S(1)} %collective-permute-done.16.refs_11_.refs_13_), channel_id=1, source_target_pairs={{1,3},{3,1},{5,7},{7,5},{8,10},{10,8},{12,14},{14,12},{17,19},{19,... | collective-permute-start | bytes 1179656 | tf_op jit(solution)/shard_map/cond/branch_1_fun/ppermute | solution.py:603
  21.2 5.8 %collective-permute-done.17.refs_12_.refs_13_ = bf16[1536,128]{1,0:T(8,128)(2,1)S(1)} collective-permute-done((bf16[1536,128]{1,0:T(8,128)(2,1)S(1)}, bf16[1536,128]{1,0:T(8,128)(2,1)S(1)}, u32[]{:S(2)}, u32[]{:S(2)}) %collective-permute-start.17) | collective-permute-done | bytes 393248 | tf_op jit(solution)/shard_map/cond/branch_1_fun/ppermute | solution.py:596
  27.1 0.9 %collective-permute-start.18 = (bf16[1536,128]{1,0:T(8,128)(2,1)S(1)}, bf16[1536,128]{1,0:T(8,128)(2,1)S(1)}, u32[]{:S(2)}, u32[]{:S(2)}) collective-permute-start(bf16[1536,128]{1,0:T(8,128)(2,1)S(1)} %collective-permute-done.17.refs_12_.refs_13_), channel_id=1, source_target_pairs={{1,3},{3,1},{5,7},{7,5},{8,10},{10,8},{12,14},{14,12},{17,19},{19,... | collective-permute-start | bytes 1179656 | tf_op jit(solution)/shard_map/cond/branch_1_fun/ppermute | solution.py:603
  27.9 0.0 collective-permute-done.20.refs_14_
  28.0 0.0 collective-permute-done.15.refs_6_.refs_8_
  28.0 3.5 %branch_1_fun.14 = (bf16[2048,512]{1,0:T(8,128)(2,1)S(1)}, bf16[480,512]{1,0:T(8,128)(2,1)S(1)}) custom-call(s32[8]{0:T(128)} %get-tuple-element.298.refs_0_.own, s32[8]{0:T(128)S(1)} %get-tuple-element.300.refs_1_, s32[3]{0:T(128)S(1)} %get-tuple-element.299.place.refs_2_, bf16[1024,512]{1,0:T(8,128)(2,1)S(1)} %copy-done.6, bf16[1024,512]{1,0:T(8,128)(2,1)} %copy-done.10, ...), custom_call_target="tpu_custom_call" | custom-call | tf_op jit(solution)/shard_map/cond/branch_1_fun/pallas_call | solution.py:477
  31.5 4.9 %collective-permute-start.21 = (bf16[480,512]{1,0:T(8,128)(2,1)S(1)}, bf16[480,512]{1,0:T(8,128)(2,1)S(1)}, u32[]{:S(2)}, u32[]{:S(2)}) collective-permute-start(bf16[480,512]{1,0:T(8,128)(2,1)S(1)} %get-tuple-element.321.a_mine), channel_id=1, source_target_pairs={{0,1},{1,0},{2,3},{3,2},{4,5},{5,4},{6,7},{7,6},{8,9},{9,8},{10,11... | collective-permute-start | bytes 1474568 | tf_op jit(solution)/shard_map/cond/branch_1_fun/ppermute | solution.py:20
  36.4 0.0 collective-permute-done.18.refs_14_
  36.5 2.4 %branch_1_fun.13 = (bf16[2048,512]{1,0:T(8,128)(2,1)S(1)}, bf16[480,512]{1,0:T(8,128)(2,1)S(1)}) custom-call(s32[8]{0:T(128)S(1)} %copy-done.43, s32[8]{0:T(128)S(1)} %get-tuple-element.300.refs_1_, s32[3]{0:T(128)S(1)} %get-tuple-element.299.place.refs_2_, bf16[480,512]{1,0:T(8,128)(2,1)S(1)} %copy-done.23, bf16[480,512]{1,0:T(8,128)(2,1)S(1)} %copy-done.24, ...), custom_call_target="tpu_custom_call" | custom-call | tf_op jit(solution)/shard_map/cond/branch_1_fun/pallas_call | solution.py:477
  38.9 3.1 %collective-permute-start.19 = (bf16[480,512]{1,0:T(8,128)(2,1)S(1)}, bf16[480,512]{1,0:T(8,128)(2,1)S(1)}, u32[]{:S(2)}, u32[]{:S(2)}) collective-permute-start(bf16[480,512]{1,0:T(8,128)(2,1)S(1)} %get-tuple-element.318.b_mine), channel_id=1, source_target_pairs={{0,1},{1,0},{2,3},{3,2},{4,5},{5,4},{6,7},{7,6},{8,9},{9,8},{10,11... | collective-permute-start | bytes 1474568 | tf_op jit(solution)/shard_map/cond/branch_1_fun/ppermute | solution.py:20
  42.0 1.2 %branch_1_fun.15.early_ref = f32[240,512]{1,0:T(8,128)S(1)} custom-call(s32[3]{0:T(128)S(1)} %get-tuple-element.299.place.refs_2_, bf16[480,512]{1,0:T(8,128)(2,1)S(1)} %get-tuple-element.321.a_mine, bf16[480,512]{1,0:T(8,128)(2,1)S(1)} %collective-permute-done.21.a_their, bf16[2048,512]{1,0:T(8,128)(2,1)S(1)} %get-tuple-element.319.ints_a), custom_call_target="tpu_custom_call" | custom-call | tf_op jit(solution)/shard_map/cond/branch_1_fun/pallas_call | solution.py:477
  43.2 1.7 %branch_1_fun.16.sym_ref = f32[240,1024]{1,0:T(8,128)S(1)} custom-call(s32[3]{0:T(128)S(1)} %get-tuple-element.299.place.refs_2_, bf16[480,512]{1,0:T(8,128)(2,1)S(1)} %get-tuple-element.321.a_mine, bf16[480,512]{1,0:T(8,128)(2,1)S(1)} %collective-permute-done.21.a_their, bf16[480,512]{1,0:T(8,128)(2,1)S(1)} %get-tuple-element.318.b_mine, ...), custom_call_target="tpu_custom_call" | custom-call | tf_op jit(solution)/shard_map/cond/branch_1_fun/pallas_call | solution.py:477
  45.0 2.2 %branch_1_fun.17 = f32[240,1024]{1,0:T(8,128)} custom-call(s32[8]{0:T(128)S(1)} %copy-done.43, s32[3]{0:T(128)S(1)} %get-tuple-element.299.place.refs_2_, bf16[480,512]{1,0:T(8,128)(2,1)S(1)} %collective-permute-done.19.b_their, bf16[2048,512]{1,0:T(8,128)(2,1)S(1)} %get-tuple-element.319.ints_a, bf16[2048,512]{1,0:T(8,128)(2,1)S(1)} %get-tuple-element.320.ints_b, ...), custom_call_target="tpu_custom_call" | custom-call | tf_op jit(solution)/shard_map/cond/branch_1_fun/pallas_call | solution.py:477
  (20 shorter events, 0.0 us)
Async XLA Ops:
  0.0 5.3 %collective-permute-start.52 = (bf16[1024,512]{1,0:T(8,128)(2,1)}, bf16[1024,512]{1,0:T(8,128)(2,1)S(1)}, u32[]{:S(2)}, u32[]{:S(2)}) collective-permute-start(bf16[1024,512]{1,0:T(8,128)(2,1)} %param.25), channel_id=1, source_target_pairs={{0,1},{1,0},{2,3},{3,2},{4,5},{5,4},{6,7},{7,6},{8,9},{9,8},{10,11... | collective-permute-start | bytes 3145736 | tf_op jit(solution)/shard_map/ppermute | solution.py:20
  0.7 2.5 %collective-permute-start.51 = (s32[8]{0:T(128)}, s32[8]{0:T(128)S(1)}, u32[]{:S(2)}, u32[]{:S(2)}) collective-permute-start(s32[8]{0:T(128)} %own.3), channel_id=1, source_target_pairs={{0,1},{1,0},{2,3},{3,2},{4,5},{5,4},{6,7},{7,6},{8,9},{9,8},{10,11... | collective-permute-start | bytes 104 | tf_op jit(solution)/shard_map/ppermute | solution.py:20
  5.4 2.8 %copy-start.10 = (bf16[1024,512]{1,0:T(8,128)(2,1)}, bf16[1024,512]{1,0:T(8,128)(2,1)S(1)}, u32[]{:S(2)}) copy-start(bf16[1024,512]{1,0:T(8,128)(2,1)S(1)} %get-tuple-element.315.their_ref.refs_4_) | copy-start | bytes 3145732 | tf_op jit(solution)/shard_map/cond
  5.4 22.6 %copy-start.6 = (bf16[1024,512]{1,0:T(8,128)(2,1)S(1)}, bf16[1024,512]{1,0:T(8,128)(2,1)}, u32[]{:S(2)}) copy-start(bf16[1024,512]{1,0:T(8,128)(2,1)} %get-tuple-element.314.mine_ref.refs_3_) | copy-start | bytes 3145732 | tf_op jit(solution)/shard_map/cond
  5.4 22.6 %copy-start.37 = (f32[1024]{0:T(1024)S(1)}, f32[1024]{0:T(1024)}, u32[]{:S(2)}) copy-start(f32[1024]{0:T(1024)} %get-tuple-element.312) | copy-start | bytes 12292 | tf_op jit(solution)/shard_map/cond
  5.4 10.4 %collective-permute-start.13 = (bf16[1568,128]{1,0:T(8,128)(2,1)S(1)}, bf16[1568,128]{1,0:T(8,128)(2,1)S(1)}, u32[]{:S(2)}, u32[]{:S(2)}) collective-permute-start(bf16[1568,128]{1,0:T(8,128)(2,1)S(1)} %get-tuple-element.303), channel_id=1, source_target_pairs={{0,2},{2,0},{1,3},{3,1},{4,6},{6,4},{5,7},{7,5},{8,10},{10,8},{9,1... | collective-permute-start | bytes 1204232 | tf_op jit(solution)/shard_map/cond/branch_1_fun/ppermute | solution.py:20
  8.2 12.3 %collective-permute-start.16 = (bf16[1536,128]{1,0:T(8,128)(2,1)S(1)}, bf16[1536,128]{1,0:T(8,128)(2,1)S(1)}, u32[]{:S(2)}, u32[]{:S(2)}) collective-permute-start(bf16[1536,128]{1,0:T(8,128)(2,1)S(1)} %get-tuple-element.316), channel_id=1, source_target_pairs={{0,4},{1,8},{4,0},{5,12},{9,13},{8,1},{13,9},{12,5},{2,6},{3,10},{... | collective-permute-start | bytes 1179656 | tf_op jit(solution)/shard_map/cond/branch_1_fun/ppermute | solution.py:596
  9.6 17.5 %collective-permute-start.17 = (bf16[1536,128]{1,0:T(8,128)(2,1)S(1)}, bf16[1536,128]{1,0:T(8,128)(2,1)S(1)}, u32[]{:S(2)}, u32[]{:S(2)}) collective-permute-start(bf16[1536,128]{1,0:T(8,128)(2,1)S(1)} %get-tuple-element.317), channel_id=1, source_target_pairs={{0,4},{1,12},{4,0},{5,8},{9,13},{8,5},{13,9},{12,1},{2,6},{3,14},{... | collective-permute-start | bytes 1179656 | tf_op jit(solution)/shard_map/cond/branch_1_fun/ppermute | solution.py:596
  15.8 20.6 %copy-start.1 = (bf16[240,1024]{1,0:T(8,128)(2,1)S(1)}, bf16[240,1024]{1,0:T(8,128)(2,1)}, u32[]{:S(2)}) copy-start(bf16[240,1024]{1,0:T(8,128)(2,1)} %get-tuple-element.307.refs_7_.refs_9_.driver) | copy-start | bytes 1474564 | tf_op jit(solution)/shard_map/cond
  15.8 20.6 %copy-start.43 = (s32[8]{0:T(128)S(1)}, s32[8]{0:T(128)}, u32[]{:S(2)}) copy-start(s32[8]{0:T(128)} %get-tuple-element.298.refs_0_.own) | copy-start | bytes 100 | tf_op jit(solution)/shard_map/cond
  19.0 17.4 %copy-start.16 = (f32[720,128]{1,0:T(8,128)S(1)}, f32[720,128]{1,0:T(8,128)}, u32[]{:S(2)}) copy-start(f32[720,128]{1,0:T(8,128)} %get-tuple-element.311.refs_9_.refs_11_.columns) | copy-start | bytes 1105924 | tf_op jit(solution)/shard_map/cond
  19.0 17.4 %copy-start.23 = (bf16[480,512]{1,0:T(8,128)(2,1)S(1)}, bf16[480,512]{1,0:T(8,128)(2,1)}, u32[]{:S(2)}) copy-start(bf16[480,512]{1,0:T(8,128)(2,1)} %get-tuple-element.308.refs_3_.refs_5_) | copy-start | bytes 1474564 | tf_op jit(solution)/shard_map/cond
  19.0 17.4 %copy-start.24 = (bf16[480,512]{1,0:T(8,128)(2,1)S(1)}, bf16[480,512]{1,0:T(8,128)(2,1)}, u32[]{:S(2)}) copy-start(bf16[480,512]{1,0:T(8,128)(2,1)} %get-tuple-element.309.refs_4_.refs_6_) | copy-start | bytes 1474564 | tf_op jit(solution)/shard_map/cond
  19.1 17.4 %copy-start.25 = (bf16[240,1024]{1,0:T(8,128)(2,1)S(1)}, bf16[240,1024]{1,0:T(8,128)(2,1)}, u32[]{:S(2)}) copy-start(bf16[240,1024]{1,0:T(8,128)(2,1)} %get-tuple-element.310.refs_8_.refs_10_) | copy-start | bytes 1474564 | tf_op jit(solution)/shard_map/cond
  19.1 8.9 %collective-permute-start.14 = (bf16[480,512]{1,0:T(8,128)(2,1)}, bf16[480,512]{1,0:T(8,128)(2,1)S(1)}, u32[]{:S(2)}, u32[]{:S(2)}) collective-permute-start(bf16[480,512]{1,0:T(8,128)(2,1)} %get-tuple-element.308.refs_3_.refs_5_), channel_id=1, source_target_pairs={{0,1},{1,0},{2,3},{3,2},{4,5},{5,4},{6,7},{7,6},{8,9},{9,8},{10,11... | collective-permute-start | bytes 1474568 | tf_op jit(solution)/shard_map/cond/branch_1_fun/ppermute | solution.py:20
  20.5 7.5 %collective-permute-start.15 = (bf16[480,512]{1,0:T(8,128)(2,1)}, bf16[480,512]{1,0:T(8,128)(2,1)S(1)}, u32[]{:S(2)}, u32[]{:S(2)}) collective-permute-start(bf16[480,512]{1,0:T(8,128)(2,1)} %get-tuple-element.309.refs_4_.refs_6_), channel_id=1, source_target_pairs={{0,1},{1,0},{2,3},{3,2},{4,5},{5,4},{6,7},{7,6},{8,9},{9,8},{10,11... | collective-permute-start | bytes 1474568 | tf_op jit(solution)/shard_map/cond/branch_1_fun/ppermute | solution.py:20
  20.6 7.4 %collective-permute-start.20 = (bf16[1536,128]{1,0:T(8,128)(2,1)S(1)}, bf16[1536,128]{1,0:T(8,128)(2,1)S(1)}, u32[]{:S(2)}, u32[]{:S(2)}) collective-permute-start(bf16[1536,128]{1,0:T(8,128)(2,1)S(1)} %collective-permute-done.16.refs_11_.refs_13_), channel_id=1, source_target_pairs={{1,3},{3,1},{5,7},{7,5},{8,10},{10,8},{12,14},{14,12},{17,19},{19,... | collective-permute-start | bytes 1179656 | tf_op jit(solution)/shard_map/cond/branch_1_fun/ppermute | solution.py:603
  27.1 9.4 %collective-permute-start.18 = (bf16[1536,128]{1,0:T(8,128)(2,1)S(1)}, bf16[1536,128]{1,0:T(8,128)(2,1)S(1)}, u32[]{:S(2)}, u32[]{:S(2)}) collective-permute-start(bf16[1536,128]{1,0:T(8,128)(2,1)S(1)} %collective-permute-done.17.refs_12_.refs_13_), channel_id=1, source_target_pairs={{1,3},{3,1},{5,7},{7,5},{8,10},{10,8},{12,14},{14,12},{17,19},{19,... | collective-permute-start | bytes 1179656 | tf_op jit(solution)/shard_map/cond/branch_1_fun/ppermute | solution.py:603
  31.5 10.5 %collective-permute-start.21 = (bf16[480,512]{1,0:T(8,128)(2,1)S(1)}, bf16[480,512]{1,0:T(8,128)(2,1)S(1)}, u32[]{:S(2)}, u32[]{:S(2)}) collective-permute-start(bf16[480,512]{1,0:T(8,128)(2,1)S(1)} %get-tuple-element.321.a_mine), channel_id=1, source_target_pairs={{0,1},{1,0},{2,3},{3,2},{4,5},{5,4},{6,7},{7,6},{8,9},{9,8},{10,11... | collective-permute-start | bytes 1474568 | tf_op jit(solution)/shard_map/cond/branch_1_fun/ppermute | solution.py:20
  38.9 6.1 %collective-permute-start.19 = (bf16[480,512]{1,0:T(8,128)(2,1)S(1)}, bf16[480,512]{1,0:T(8,128)(2,1)S(1)}, u32[]{:S(2)}, u32[]{:S(2)}) collective-permute-start(bf16[480,512]{1,0:T(8,128)(2,1)S(1)} %get-tuple-element.318.b_mine), channel_id=1, source_target_pairs={{0,1},{1,0},{2,3},{3,2},{4,5},{5,4},{6,7},{7,6},{8,9},{9,8},{10,11... | collective-permute-start | bytes 1474568 | tf_op jit(solution)/shard_map/cond/branch_1_fun/ppermute | solution.py:20
